TPU v7x, 128 devices: a whole 4x4x4 slice. The times are simulated.
128 devices in a mesh: row: 8 (over x, core), col: 16 (over z, y).
Axes of the slice: x: 4, y: 4, z: 4, core: 2. Of those that a mesh axis runs over, the one named last changes fastest.
Arguments:
- values: bfloat16 [1024, 60416], P('col', 'row'), as said below
- pattern: int32 [944, 16], P(None, 'col'), may hold values from 0 to 943, as said below
Outputs:
- squared: bfloat16 [1024, 60416], P('col', 'row')
- updated: bfloat16 [1024, 60416], P('col', 'row')
Inputs may be any that keep to these rules, and one draw needn't show every extreme that they name: pattern[r, g] lies in the group g * 59 to (g + 1) * 59 - 1; pattern[r, r // 59] = r; the pattern is symmetric: pattern[pattern[r, g], r // 59] = r. values define a symmetric matrix: the block stored for block row r in group g is exactly the transpose of the block stored for block row pattern[r, g] in group r // 59.
All inputs are finite; a program needn't handle non-finite values.
Results may differ from a plain program's by a relative error of at most 0.0047.
Values may be sent and summed in bfloat16 or wider, within the bound.
No kernel may reach another device: no remote copies, remote signals or barrier semaphores. Data moves between devices by JAX's collectives and lax.ppermute only.
A program may use at most 320 MiB of HBM per device.

v0:
```python
import math

import jax
import jax.numpy as jnp
from jax import lax
from jax.sharding import PartitionSpec as P


def summed_partials(right, masked_panel, panel_links, total_rows):
    block_size = right.shape[0]
    rows_here = right.shape[1] // block_size
    strips = right.reshape(block_size, rows_here, block_size)
    products = jnp.einsum(
        "qkt,gpkt->kgqp", strips, masked_panel, preferred_element_type=jnp.float32
    )
    flattened = products.reshape(rows_here * panel_links.shape[1], block_size, block_size)
    partial_sum = jnp.zeros((total_rows, block_size, block_size), jnp.float32)
    partial_sum = partial_sum.at[panel_links.reshape(-1)].add(flattened)
    mine = lax.psum_scatter(partial_sum, "row", scatter_dimension=0, tiled=True)
    return jnp.transpose(mine, (1, 0, 2)).reshape(block_size, rows_here * block_size)


def block_product(right, masked_panel, panel_links, total_rows):
    return summed_partials(right, masked_panel, panel_links, total_rows)


def per_device(values, pattern):
    block_size = values.shape[0]
    rows_here = values.shape[1] // block_size
    groups = lax.axis_size("col")
    first_row = lax.axis_index("row") * rows_here
    column = pattern[:, 0]
    total_rows = column.shape[0]
    own_links = lax.dynamic_slice_in_dim(pattern, first_row, rows_here, 0)
    panel_values, panel_links = (
        lax.all_gather(values, "col", axis=0, tiled=True),
        lax.all_gather(own_links, "col", axis=1, tiled=True),
    )
    gathered = panel_values.reshape(groups, block_size, rows_here, block_size)
    targets = lax.dynamic_slice_in_dim(column, first_row, rows_here, 0)
    kept_mask = jnp.take(column, panel_links, axis=0) == targets[:, None]
    masked_panel = jnp.where(kept_mask.T[:, None, :, None], gathered, jnp.zeros((), gathered.dtype))
    norm_scale = math.sqrt(groups * block_size)
    first_sum = block_product(values, masked_panel, panel_links, total_rows)
    squared = (first_sum / norm_scale).astype(jnp.bfloat16)
    second = block_product(squared, masked_panel, panel_links, total_rows)
    updated = (1.5 * values.astype(jnp.float32) - 0.5 * second / norm_scale).astype(jnp.bfloat16)
    return (squared, updated)


def solution(mesh):
    in_specs = (P("col", "row"), P(None, "col"))
    out_specs = (P("col", "row"), P("col", "row"))
    return jax.shard_map(
        per_device, mesh=mesh, in_specs=in_specs, out_specs=out_specs, check_vma=False
    )
```

profile of v0, /device:TPU:1, one launch (start us, length us, event | category | flops | bytes accessed | tf_op | source)
XLA Modules:
  0.0 1370.0 jit_solution(6549942981248730659)
XLA Ops:
  7.2 0.0 copy-start
  7.2 0.0 all-gather.3.cloned.1.call-start
  7.2 0.7 all-gather.3.cloned.1.call-update
  7.9 0.0 reduce-scatter.3.cloned.1.call-start
  8.0 2.9 reshape.66
  10.8 0.8 fusion.7
  11.6 18.7 %all-gather = s32[16,1,118]{2,1,0:T(1,128)S(1)} all-gather(s32[1,1,118]{2,1,0:T(1,128)S(1)} %get-tuple-element.3), channel_id=1, replica_groups=mesh['row'=8,'col'=16] {'col'}, dimensions={0}, use_global_device_ids=true | all-gather | bytes 8024 | tf_op jit(solution)/shard_map/all_gather | solution.py:37
  30.3 0.1 copy.23
  30.4 0.1 reshape.71
  30.5 0.0 copy-done
  30.5 7.2 gather_fusion
  37.8 0.1 reshape.70
  37.8 0.1 reshape.64
  38.0 0.1 fusion.5
  38.1 80.1 %all-gather.3.cloned.1.call-done = bf16[1024,7552]{1,0:T(8,128)(2,1)} async-done(((bf16[64,7552]{1,0:T(8,128)(2,1)}), bf16[1024,7552]{1,0:T(8,128)(2,1)}) %all-gather.3.cloned.1.call-update) | async-done | bytes 15466512 | tf_op jit(solution)/shard_map/all_gather | solution.py:36
  118.1 20.5 %copy.24 = bf16[1024,7552]{0,1:T(8,128)(2,1)} copy(bf16[1024,7552]{1,0:T(8,128)(2,1)} %all-gather.3.cloned.1.call-done) | data formatting | bytes 30932992 | tf_op jit(solution)/shard_map/all_gather | solution.py:36
  138.6 39.8 %reshape.65 = bf16[16,64,118,64]{1,0,3,2:T(8,128)(2,1)} reshape(bf16[1024,7552]{0,1:T(8,128)(2,1)} %copy.24) | data formatting | bytes 30932992 | tf_op jit(solution)/shard_map/reshape | solution.py:39
  178.4 21.0 %broadcast_select_fusion = bf16[16,64,118,64]{1,0,3,2:T(8,128)(2,1)} fusion(bf16[16,64,118,64]{1,0,3,2:T(8,128)(2,1)} %reshape.65, pred[16,118]{0,1:T(8,128)(4,1)S(1)} %fusion.5), kind=kLoop, calls=%fused_computation.3 | loop fusion | flops 7733248 | bytes 30934880 | tf_op jit(solution)/shard_map/jit(_where)/select_n | solution.py:42
  199.4 42.3 %copy.25 = bf16[16,64,118,64]{3,1,0,2:T(8,128)(2,1)} copy(bf16[16,64,118,64]{1,0,3,2:T(8,128)(2,1)} %broadcast_select_fusion) | data formatting | bytes 30932992 | tf_op jit(solution)/shard_map/jit(_where)/select_n | solution.py:42
  241.6 31.0 %fusion.2 = f32[118,16,64,64]{3,2,1,0:T(8,128)} fusion(bf16[16,64,118,64]{3,1,0,2:T(8,128)(2,1)} %copy.25, bf16[64,118,64,1]{2,1,0,3:T(8,128)(2,1)S(1)} %bitcast.37), kind=kOutput, calls=%fused_computation.8 | convolution fusion | flops 989855744 | bytes 47366144 | tf_op jit(solution)/shard_map/qkt,gpkt->kgqp/dot_general | solution.py:13
  272.6 60.7 %copy.27 = f32[1888,64,64]{2,1,0:T(8,128)} copy(f32[1888,64,64]{1,2,0:T(8,128)} %bitcast.35) | data formatting | bytes 61865984 | tf_op jit(solution)/shard_map/reshape | solution.py:16
  333.3 14.2 %broadcast.43.clone = f32[944,64,64]{2,1,0:T(8,128)} broadcast(f32[]{:T(128)} %constant.12.clone.1), dimensions={} | broadcast | bytes 15466500 | tf_op jit(solution)/shard_map/broadcast.7
  347.5 290.4 %scatter_fusion = f32[944,64,64]{2,1,0:T(8,128)} fusion(f32[944,64,64]{2,1,0:T(8,128)} %broadcast.43.clone, s32[1888]{0:T(1024)S(1)} %fusion.6, f32[1888,64,64]{2,1,0:T(8,128)} %copy.27), kind=kCustom, calls=%fused_computation.1 | custom fusion | flops 7733248 | bytes 92806528 | tf_op jit(solution)/shard_map/scatter-add | solution.py:18
  637.8 0.0 reduce-scatter.3.cloned.1.call-update
  637.8 0.2 reduce-scatter.5.cloned.1.call-start
  638.1 157.4 %reduce-scatter.3.cloned.1.call-done = f32[118,64,64]{2,1,0:T(8,128)} async-done(((f32[944,64,64]{2,1,0:T(8,128)}), f32[118,64,64]{2,1,0:T(8,128)}) %reduce-scatter.3.cloned.1.call-update) | async-done | bytes 1933328 | tf_op jit(solution)/shard_map/reduce_scatter | solution.py:19
  795.5 33.7 %fusion = f32[118,16,64,64]{3,2,1,0:T(8,128)} fusion(bf16[16,64,118,64]{3,1,0,2:T(8,128)(2,1)} %copy.25, f32[118,64,64]{2,1,0:T(8,128)} %reduce-scatter.3.cloned.1.call-done), kind=kOutput, calls=%fused_computation.6 | convolution fusion | flops 990822400 | bytes 48332800 | tf_op jit(solution)/shard_map/qkt,gpkt->kgqp/dot_general | solution.py:13
  829.1 60.7 %copy.30 = f32[1888,64,64]{2,1,0:T(8,128)} copy(f32[1888,64,64]{1,2,0:T(8,128)} %bitcast.36) | data formatting | bytes 61865984 | tf_op jit(solution)/shard_map/reshape | solution.py:16
  889.8 14.2 %broadcast.43 = f32[944,64,64]{2,1,0:T(8,128)} broadcast(f32[]{:T(128)} %constant.12.clone.1), dimensions={} | broadcast | bytes 15466500 | tf_op jit(solution)/shard_map/broadcast.7
  904.0 290.4 %scatter_fusion.1 = f32[944,64,64]{2,1,0:T(8,128)} fusion(f32[944,64,64]{2,1,0:T(8,128)} %broadcast.43, s32[1888]{0:T(1024)S(1)} %fusion.6, f32[1888,64,64]{2,1,0:T(8,128)} %copy.30), kind=kCustom, calls=%fused_computation.2 | custom fusion | flops 7733248 | bytes 92806528 | tf_op jit(solution)/shard_map/scatter-add | solution.py:18
  1194.3 0.0 reduce-scatter.5.cloned.1.call-update
  1194.4 2.6 fusion.4
  1197.0 0.0 copy-start.1
  1197.0 1.3 copy.28
  1198.3 2.0 convert_element_type.19
  1200.2 152.1 %reduce-scatter.5.cloned.1.call-done = f32[118,64,64]{2,1,0:T(8,128)} async-done(((f32[944,64,64]{2,1,0:T(8,128)}), f32[118,64,64]{2,1,0:T(8,128)}) %reduce-scatter.5.cloned.1.call-update) | async-done | bytes 1933328 | tf_op jit(solution)/shard_map/reduce_scatter | solution.py:19
  1352.4 2.6 multiply_bitcast_fusion
  1355.0 4.1 copy.31
  1359.1 3.2 div.16
  1362.3 0.0 copy-done.1
  1362.3 1.2 subtract_convert_fusion
  (3 shorter events, 0.0 us)
Async XLA Ops:
  7.2 23.4 %copy-start = (s32[944,1]{0,1:T(1,128)S(1)}, s32[944,1]{0,1:T(1,128)}, u32[]{:S(2)}) copy-start(s32[944,1]{0,1:T(1,128)} %param.3) | copy-start | bytes 11332
  7.2 111.0 %all-gather.3.cloned.1.call-start = ((), (), s32[]{:S(2)}) async-start(), calls=%async_computation.2 | async-start | bytes 16433152 | tf_op jit(solution)/shard_map/all_gather | solution.py:36
  7.9 787.6 %reduce-scatter.3.cloned.1.call-start = ((), (), s32[]{:S(2)}) async-start(), calls=%async_computation.3 | async-start | bytes 34799616 | tf_op jit(solution)/shard_map/reduce_scatter | solution.py:19
  637.8 714.5 %reduce-scatter.5.cloned.1.call-start = ((), (), s32[]{:S(2)}) async-start(), calls=%async_computation.4 | async-start | bytes 34799616 | tf_op jit(solution)/shard_map/reduce_scatter | solution.py:19
  1197.0 165.3 %copy-start.1 = (bf16[64,7552]{1,0:T(8,128)(2,1)S(1)}, bf16[64,7552]{1,0:T(8,128)(2,1)}, u32[]{:S(2)}) copy-start(bf16[64,7552]{1,0:T(8,128)(2,1)} %param.2) | copy-start | bytes 2899972
Sparse Core Ops, SparseCore 0:
  10.2 107.9 all-gather.2
  638.0 157.4 reduce-scatter.2
  1194.5 157.8 reduce-scatter.4
where the time goes:
time: 1380 us; the launch traced here: 1370 us
  other arithmetic  608 us (44%)
  waiting for transfers between devices  390 us (28%)
  local copies, waits for them, and re-layouts  274 us (20%)
  matrix products  64.7 us (5%)
  blocking collectives  18.7 us (1%)
  between operations  13.9 us (1%)
    scatter-add x2, other arithmetic, summed_partials(): partial_sum = partial_sum.at[panel_links.reshape(-1)].add(flattened)  581 us
    reduce_scatter x2, waiting for transfers between devices, summed_partials(): mine = lax.psum_scatter(partial_sum, 'row', scatter_dimension=0, tiled=True)  310 us
    reshape x2, local copies, waits for them, and re-layouts, summed_partials(): products.reshape(rows_here * panel_links.shape[1], block_size, block_size)  121 us
    all_gather x1, waiting for transfers between devices, per_device(): lax.all_gather(values, 'col', axis=0, tiled=True)  80.1 us
    dot_general x2, matrix products, summed_partials(): jnp.einsum('qkt,gpkt->kgqp', strips, masked_panel, preferred_element_type...  64.7 us
    select_n x1, local copies, waits for them, and re-layouts, per_device(): jnp.where(kept_mask.T[:, None, :, None], gathered, jnp.zeros((), gathered...  42.3 us
    reshape x1, local copies, waits for them, and re-layouts, per_device(): gathered = panel_values.reshape(groups, block_size, rows_here, block_size)  39.8 us
    another operation x2, local copies, waits for them, and re-layouts  28.3 us
  transfers between devices with their start and end apart: 3, of which 3 were waited for; matrix products, arithmetic and copies ran while one was open for 1% of the time, Pallas kernels for 0%

commit v1 on v0

v1 whole, which is shorter than its diff:
```python
import math

import jax
import jax.numpy as jnp
from jax import lax
from jax.experimental import pallas as pl
from jax.experimental.pallas import tpu as pltpu
from jax.sharding import PartitionSpec as P

STEPS = 4


def split_pairs(flat_ref, pair_ref, block):
    spans = pair_ref.shape[0]
    for m in range(spans):
        pair_ref[m, :, :block] = flat_ref[:, m * block : (m + 1) * block]
        pair_ref[m, :, block:] = flat_ref[:, (spans + m) * block : (spans + m + 1) * block]


def join_pairs(pair_ref, flat_ref, block):
    spans = pair_ref.shape[0]
    for m in range(spans):
        flat_ref[:, m * block : (m + 1) * block] = pair_ref[m, :, :block]
        flat_ref[:, (spans + m) * block : (spans + m + 1) * block] = pair_ref[m, :, block:]


def paired(array, spans):
    block = array.shape[0]

    def body(flat_ref, pair_ref):
        split_pairs(flat_ref, pair_ref, block)

    return pl.pallas_call(
        body,
        out_shape=jax.ShapeDtypeStruct((spans, block, 2 * block), array.dtype),
        compiler_params=pltpu.CompilerParams(vmem_limit_bytes=16 * 1024 * 1024),
    )(array)


def product_kernel(left_at, right_at, kept, left_ref, right_ref, *rest, block, scale, update):
    if update:
        own_ref, flat_ref, out_ref, total = rest
    else:
        flat_ref, out_ref, total = rest
    step = pl.program_id(0)
    spans = total.shape[0]
    pairs = left_ref.shape[0]
    groups = right_ref.shape[0]
    low = lax.broadcasted_iota(jnp.int32, (block, 2 * block), 1) < block

    def one(s, carry):
        left_parts = []
        for j in range(pairs):
            base = s * (STEPS * groups) + step * groups + 2 * j
            left_parts.append(jnp.where(low, left_ref[j, left_at[base]], left_ref[j, left_at[base + 1]]))
        left = jnp.concatenate(left_parts, axis=1)
        first, second = right_at[2 * s], right_at[2 * s + 1]
        right_parts = []
        for h in range(groups):
            flag = (s * (STEPS * groups) + step * groups + h) * 2
            picked = jnp.where(low, right_ref[h, first], right_ref[h, second])
            keep = jnp.where(low, kept[flag], kept[flag + 1]) != 0
            right_parts.append(jnp.where(keep, picked, jnp.zeros_like(picked)))
        right = jnp.concatenate(right_parts, axis=0)
        partial = jnp.dot(left, right, preferred_element_type=jnp.float32)

        @pl.when(step == 0)
        def _():
            total[s] = partial

        @pl.when(jnp.logical_and(step > 0, step < STEPS - 1))
        def _():
            total[s] += partial

        @pl.when(step == STEPS - 1)
        def _():
            summed = total[s] + partial
            if update:
                own = jnp.where(low, own_ref[first], own_ref[second]).astype(jnp.float32)
                result = (1.5 * own - (0.5 * scale) * summed).astype(out_ref.dtype)
            else:
                result = (summed * scale).astype(out_ref.dtype)
            out_ref[first, :, :block] = result[:, :block]
            out_ref[second, :, block:] = result[:, block:]

        return carry

    lax.fori_loop(0, spans, one, 0)

    @pl.when(step == STEPS - 1)
    def _():
        join_pairs(out_ref, flat_ref, block)


def product(left_at, right_at, kept, left, right, own, scale):
    pairs, spans, block, lanes = left.shape
    groups = right.shape[0]
    whole = pl.BlockSpec((spans, block, lanes), lambda i, *_: (0, 0, 0))
    flat = pl.BlockSpec((block, spans * lanes), lambda i, *_: (0, 0))
    in_specs = [
        pl.BlockSpec((pairs // STEPS, spans, block, lanes), lambda i, *_: (i, 0, 0, 0)),
        pl.BlockSpec((groups // STEPS, spans, block, lanes), lambda i, *_: (i, 0, 0, 0)),
    ]
    out_specs = [flat]
    out_shape = [jax.ShapeDtypeStruct((block, spans * lanes), jnp.bfloat16)]
    scratch_shapes = [pltpu.VMEM((spans, block, lanes), jnp.float32)]
    operands = [left, right]
    if own is not None:
        in_specs.append(whole)
        operands.append(own)
        scratch_shapes.insert(0, pltpu.VMEM((spans, block, lanes), jnp.bfloat16))
    else:
        out_specs.append(whole)
        out_shape.append(jax.ShapeDtypeStruct((spans, block, lanes), jnp.bfloat16))

    def body(*refs):
        product_kernel(*refs, block=block, scale=scale, update=own is not None)

    return pl.pallas_call(
        body,
        grid_spec=pltpu.PrefetchScalarGridSpec(
            num_scalar_prefetch=3,
            grid=(STEPS,),
            in_specs=in_specs,
            out_specs=out_specs,
            scratch_shapes=scratch_shapes,
        ),
        out_shape=out_shape,
        compiler_params=pltpu.CompilerParams(
            dimension_semantics=("arbitrary",), vmem_limit_bytes=48 * 1024 * 1024
        ),
        cost_estimate=pl.CostEstimate(
            flops=2 * spans * block * lanes * groups * block,
            bytes_accessed=2 * (left.size + right.size),
            transcendentals=0,
        ),
    )(left_at, right_at, kept, *operands)


def per_device(values, pattern):
    block = values.shape[0]
    rows_here = values.shape[1] // block
    groups = lax.axis_size("col")
    spans = pattern.shape[0] // groups
    mine = lax.axis_index("row")
    group = lax.axis_index("col")
    column = pattern[:, 0]

    own = paired(values, spans)
    own_links = lax.dynamic_slice_in_dim(column, mine * rows_here, rows_here, 0)
    links = lax.all_gather(own_links, "col", axis=0, tiled=False)
    left = lax.all_gather(own, "row", axis=0, tiled=False)
    right = lax.all_gather(own, "col", axis=0, tiled=False)

    order = jnp.arange(rows_here, dtype=jnp.int32) % spans
    targets = (own_links - group * spans).reshape(2, spans)
    member = jnp.arange(spans, dtype=jnp.int32)
    inverse = jnp.sum(
        jnp.where(targets[:, :, None] == member[None, None, :], member[None, :, None], 0), axis=1
    )
    right_at = inverse.T.reshape(-1).astype(jnp.int32)
    flags = (jnp.take(column, links, axis=0) == own_links[None, :]).astype(jnp.int32)
    flags = flags.reshape(groups, 2, spans)
    kept = jnp.stack([jnp.take(flags[:, e], inverse[e], axis=1) for e in range(2)], axis=-1)
    kept = kept.transpose(1, 0, 2).reshape(-1)
    by_group = (column - group * spans).reshape(groups, spans)
    left_at = jnp.sum(
        jnp.where(by_group[:, :, None] == member[None, None, :], member[None, :, None], 0), axis=1
    )
    left_at = left_at.T.reshape(-1).astype(jnp.int32)

    scale = 1.0 / math.sqrt(groups * block)
    squared, square_pairs = product(left_at, right_at, kept, left, right, None, scale)
    left = lax.all_gather(square_pairs, "row", axis=0, tiled=False)
    (updated,) = product(left_at, right_at, kept, left, right, own, scale)
    return (squared, updated)


def solution(mesh):
    in_specs = (P("col", "row"), P(None, "col"))
    out_specs = (P("col", "row"), P("col", "row"))
    return jax.shard_map(
        per_device, mesh=mesh, in_specs=in_specs, out_specs=out_specs, check_vma=False
    )
```

time: 1380 us -> 302 us (0.22)
  other arithmetic: 608 us -> 1.24 us
  local copies, waits for them, and re-layouts: 274 us -> 14.4 us
  waiting for transfers between devices: 390 us -> 174 us
  Pallas kernels: 0 us -> 82.3 us
  matrix products: 64.7 us -> 0 us
    scatter-add x2 -> x0, other arithmetic: 581 us -> none  [summed_partials(): partial_sum = partial_sum.at[panel_links.reshape(-1)].add(flattened)]
    reduce_scatter x2 -> x0, waiting for transfers between devices: 310 us -> none  [summed_partials(): mine = lax.psum_scatter(partial_sum, 'row', scatter_dimension=0, tiled=True)]
    reshape x5 -> x3, local copies, waits for them, and re-layouts: 164 us -> 0.47 us  [the longest x1 0.25 us: per_device(): kept = kept.transpose(1, 0, 2).reshape(-1)]
    all_gather x1 -> x3, waiting for transfers between devices: 80.1 us -> 173 us  [the longest x1 107 us: per_device(): right = lax.all_gather(own, 'col', axis=0, tiled=False)]
    pallas_call x0 -> x3, Pallas kernels: none -> 82.3 us  [the longest x2 80.7 us: product(): pl.pallas_call(body, grid_spec=pltpu.PrefetchScalarGridSpec(num_scalar_pr...]
    dot_general x2 -> x0, matrix products: 64.7 us -> none  [summed_partials(): jnp.einsum('qkt,gpkt->kgqp', strips, masked_panel, preferred_element_type...]
    select_n x1 -> x2, local copies, waits for them, and re-layouts: 42.3 us -> 0.19 us  [per_device(): jnp.take(column, links, axis=0) == own_links[None, :]]
    another operation x2, local copies, waits for them, and re-layouts: 28.3 us -> 0.14 us  [per_device(): jnp.stack([jnp.take(flags[:, e], inverse[e], axis=1) for e in range(2)],...]
  transfers between devices with their start and end apart: 3 -> 3, of which waited for: 3 -> 3; matrix products, arithmetic and copies ran while one was open for 1% -> 5% of each run, Pallas kernels for 0% -> 0%
where the time goes in v1:
time: 302 us
  waiting for transfers between devices  174 us (58%)
  Pallas kernels  82.3 us (27%)
  blocking collectives  15 us (5%)
  between operations  14.6 us (5%)
  local copies, waits for them, and re-layouts  14.4 us (5%)
    all_gather x1, waiting for transfers between devices, per_device(): right = lax.all_gather(own, 'col', axis=0, tiled=False)  107 us
    pallas_call x2, Pallas kernels, product(): pl.pallas_call(body, grid_spec=pltpu.PrefetchScalarGridSpec(num_scalar_pr...  80.7 us
    all_gather x1, waiting for transfers between devices, per_device(): left = lax.all_gather(square_pairs, 'row', axis=0, tiled=False)  47.1 us
    all_gather x1, waiting for transfers between devices, per_device(): left = lax.all_gather(own, 'row', axis=0, tiled=False)  19.6 us
    unnamed x1, blocking collectives  15 us
    gather x2, local copies, waits for them, and re-layouts, per_device(): jnp.take(column, links, axis=0) == own_links[None, :]  7.3 us
  transfers between devices with their start and end apart: 3, of which 3 were waited for; matrix products, arithmetic and copies ran while one was open for 5% of the time, Pallas kernels for 0%

profile of v1, /device:TPU:1, one launch (start us, length us, event | category | flops | bytes accessed | tf_op | source)
XLA Modules:
  0.0 301.8 jit_solution(7427821821773191585)
XLA Ops:
  7.2 0.0 all-gather.8.cloned.1.call-start
  7.2 0.0 copy-start
  7.2 1.2 copy-done
  8.4 0.0 copy-start.1
  8.4 1.6 shard_map.41.refs_5_
  10.0 0.0 all-gather.8.cloned.1.call-update
  10.0 0.0 all-gather.10.cloned.1.call-start
  10.1 0.7 all-gather.10.cloned.1.call-update
  10.8 0.0 all-gather.12.cloned.1.call-start
  10.9 0.8 fusion.1
  11.6 0.1 dynamic_slice.6
  11.7 0.7 subtract_reduce_fusion
  12.4 0.1 sub.25
  12.5 1.2 dynamic-slice.1
  14.4 0.9 bitcast_dynamic-update-slice_fusion
  15.3 15.0 %all-reduce = s32[1888]{0:T(1024)S(1)} all-reduce(s32[1888]{0:T(1024)S(1)} %bitcast_dynamic-update-slice_fusion), channel_id=2, replica_groups=mesh['row'=8,'col'=16] {'col'}, use_global_device_ids=true, to_apply=%add | all-reduce | flops 1888 | bytes 15104
  30.3 0.1 reshape.75
  30.4 0.1 reshape.69
  30.5 0.0 copy-done.1
  30.5 7.2 %gather_fusion = s32[1888]{0:T(1024)S(1)} fusion(s32[944]{0:T(1024)S(1)} %bitcast.29, s32[2048]{0:T(1024)S(1)} %pad_clamp_fusion), kind=kCustom, calls=%fused_computation.2 | custom fusion | bytes 22656 | tf_op jit(solution)/shard_map/jit(_take)/gather | solution.py:162
  37.7 0.1 reshape.68
  37.8 0.1 select_n.36
  37.9 0.1 copy.13
  38.0 0.2 select_reduce_fusion
  38.2 0.1 copy.14
  38.3 0.1 reshape.48.refs_0_
  38.4 0.1 copy.15
  38.5 0.1 fusion
  38.6 0.1 copy.16
  38.8 0.1 reshape.49.refs_1_
  38.9 0.1 copy.17
  39.0 0.1 compare_convert_fusion
  39.1 0.6 gather_fusion.1
  39.7 0.6 gather_fusion.2
  40.3 0.1 select_bitcast_fusion
  40.4 0.1 copy.19
  40.5 0.1 copy.18
  40.6 0.3 copy.20
  40.9 0.3 reshape.50.refs_2_
  41.2 19.6 %all-gather.8.cloned.1.call-done = bf16[472,64,128]{2,1,0:T(8,128)(2,1)} async-done(((bf16[59,64,128]{2,1,0:T(8,128)(2,1)}), bf16[472,64,128]{2,1,0:T(8,128)(2,1)}) %all-gather.8.cloned.1.call-update) | async-done | bytes 7733264 | tf_op jit(solution)/shard_map/all_gather | solution.py:152
  60.8 106.6 %all-gather.10.cloned.1.call-done = bf16[944,64,128]{2,1,0:T(8,128)(2,1)} async-done(((bf16[59,64,128]{2,1,0:T(8,128)(2,1)}), bf16[944,64,128]{2,1,0:T(8,128)(2,1)}) %all-gather.10.cloned.1.call-update) | async-done | bytes 15466512 | tf_op jit(solution)/shard_map/all_gather | solution.py:153
  167.4 40.2 %shard_map.42 = (bf16[64,7552]{1,0:T(8,128)(2,1)}, bf16[59,64,128]{2,1,0:T(8,128)(2,1)}) custom-call(s32[944]{0:T(1024)S(1)} %reshape.48.refs_0_, s32[118]{0:T(128)S(1)} %reshape.49.refs_1_, s32[1888]{0:T(1024)S(1)} %reshape.50.refs_2_, bf16[8,59,64,128]{3,2,1,0:T(8,128)(2,1)} %bitcast.33, bf16[16,59,64,128]{3,2,1,0:T(8,128)(2,1)} %bitcast.30), custom_call_target="tpu_custom_call" | custom-call | flops 989855744 | bytes 23199744 | tf_op jit(solution)/shard_map/pallas_call | solution.py:119
  207.7 0.0 all-gather.12.cloned.1.call-update
  207.7 47.1 %all-gather.12.cloned.1.call-done = bf16[472,64,128]{2,1,0:T(8,128)(2,1)} async-done(((bf16[59,64,128]{2,1,0:T(8,128)(2,1)}), bf16[472,64,128]{2,1,0:T(8,128)(2,1)}) %all-gather.12.cloned.1.call-update) | async-done | bytes 7733264 | tf_op jit(solution)/shard_map/all_gather | solution.py:174
  254.8 40.5 %shard_map.43 = bf16[64,7552]{1,0:T(8,128)(2,1)} custom-call(s32[944]{0:T(1024)S(1)} %reshape.48.refs_0_, s32[118]{0:T(128)S(1)} %reshape.49.refs_1_, s32[1888]{0:T(1024)S(1)} %reshape.50.refs_2_, bf16[8,59,64,128]{3,2,1,0:T(8,128)(2,1)} %bitcast.32, bf16[16,59,64,128]{3,2,1,0:T(8,128)(2,1)} %bitcast.31, bf16[59,64,128]{2,1,0:T(8,128)(2,1)} %shard_map.41.refs_5_), custom_call_target="tpu_custom_call" | custom-call | flops 989855744 | bytes 23199744 | tf_op jit(solution)/shard_map/pallas_call | solution.py:119
  (10 shorter events, 0.1 us)
Async XLA Ops:
  7.2 53.6 %all-gather.8.cloned.1.call-start = ((), (), s32[]{:S(2)}) async-start(), calls=%async_computation | async-start | bytes 8699904 | tf_op jit(solution)/shard_map/all_gather | solution.py:152
  7.2 1.2 copy-start
  8.4 22.1 %copy-start.1 = (s32[944,1]{0,1:T(1,128)S(1)}, s32[944,1]{0,1:T(1,128)}, u32[]{:S(2)}) copy-start(s32[944,1]{0,1:T(1,128)} %param.5) | copy-start | bytes 11332
  10.0 157.4 %all-gather.10.cloned.1.call-start = ((), (), s32[]{:S(2)}) async-start(), calls=%async_computation.1 | async-start | bytes 16433152 | tf_op jit(solution)/shard_map/all_gather | solution.py:153
  10.8 244.0 %all-gather.12.cloned.1.call-start = ((), (), s32[]{:S(2)}) async-start(), calls=%async_computation.2 | async-start | bytes 8699904 | tf_op jit(solution)/shard_map/all_gather | solution.py:174
Sparse Core Ops, SparseCore 0:
  10.2 50.5 all-gather.7
  62.9 104.4 all-gather.9
  207.8 46.9 all-gather.11
